TPU v7x, 32 devices: a whole 2x2x4 slice. The times are simulated.
32 devices in a mesh: req: 8 (over z, x), mlp: 4 (over y, core).
Axes of the slice: x: 2, y: 2, z: 4, core: 2. Of those that a mesh axis runs over, the one named last changes fastest.
Arguments:
- hidden_in: bfloat16 [1024, 4096], P('req'), may hold values from -6 to 6
- attn_gain: bfloat16 [4096], replicated, may hold values from 0.5 to 1.5
- w_query: bfloat16 [4096, 2048], P(None, 'mlp'), may hold values from -0.09375 to 0.09375
- w_key: bfloat16 [4096, 512], P(None, 'mlp'), may hold values from -0.09375 to 0.09375
- w_value: bfloat16 [4096, 512], P(None, 'mlp'), may hold values from -0.09375 to 0.09375
- w_out: bfloat16 [2048, 4096], P('mlp'), may hold values from -0.125 to 0.125
- mlp_gain: bfloat16 [4096], replicated, may hold values from 0.5 to 1.5
- w_gate: bfloat16 [4096, 14336], P('mlp', 'req'), may hold values from -0.09375 to 0.09375
- w_up: bfloat16 [4096, 14336], P('mlp', 'req'), may hold values from -0.09375 to 0.09375
- w_down: bfloat16 [14336, 4096], P('req', 'mlp'), may hold values from -0.046875 to 0.046875
- prefix_kv: bfloat16 [16384, 2, 512], P('req', None, 'mlp'), may hold values from -512 to 512
- suffix_lengths: int32 [8, 4], P('req'), may hold values from 1 to 125, as said below
- prefix_owner: int32 [2, 4], replicated, may hold values from 0 to 3, each once within a row
Outputs:
- hidden_out: bfloat16 [1024, 4096], P('req', 'mlp')
- suffix_kv: bfloat16 [1024, 2, 512], P('req', None, 'mlp')
Inputs may be any that keep to these rules, and one draw needn't show every extreme that they name: `suffix_lengths`: the lengths of one index of req sum to at most 128; in every draw some index sums to exactly 128. `prefix_owner`: each row is a permutation.
All inputs are finite; a program needn't handle non-finite values.
Results may differ from a plain program's by a relative error of at most 0.02.
The roundings to bfloat16 on the way count: a program that leaves them out, or rounds other values in their place, can miss the bound.
Values may be sent and summed in bfloat16 or wider, within the bound.
A program may use at most 128 MiB of HBM per device.

v0:
```python
import functools
import math

import jax
import jax.numpy as jnp
from jax import lax
from jax.experimental import pallas as pl
from jax.experimental.pallas import tpu as pltpu
from jax.sharding import PartitionSpec as P

HEAD_DIM = 128
PREFIX = 8192
GSPAN = 4


rope_base = 500000.0
eps = 1e-05


def from_xor(value, axis, mask):
    pairs = [(source, source ^ mask) for source in range(lax.axis_size(axis))]
    return lax.ppermute(value, axis, pairs)


def rope(values, positions):
    half = values.shape[-1] // 2
    freq = rope_base ** (-jnp.arange(half, dtype=jnp.float32) * 2.0 / values.shape[-1])
    angle = positions.astype(jnp.float32)[:, None] * freq[None, :]
    cosine = jnp.cos(angle)[:, None, :]
    sine = jnp.sin(angle)[:, None, :]
    former = values[..., :half]
    latter = values[..., half:]
    return jnp.concatenate(
        [former * cosine - latter * sine, latter * cosine + former * sine], axis=-1
    )


def rms_norm(values, gain):
    return (
        values
        * lax.rsqrt(jnp.mean(values * values, axis=-1, keepdims=True) + eps)
        * gain.astype(jnp.float32)
    )


def slot_layout(lengths, slot_count):
    ends = jnp.cumsum(lengths)
    starts = ends - lengths
    slot_ids = jnp.arange(slot_count, dtype=jnp.int32)
    request_of = jnp.sum((slot_ids[:, None] >= ends[None, :]).astype(jnp.int32), axis=1)
    picks = (request_of[:, None] == jnp.arange(lengths.shape[0], dtype=jnp.int32)[None, :]).astype(
        jnp.int32
    )
    start_of = jnp.sum(picks * starts[None, :], axis=1)
    positions = PREFIX + slot_ids - start_of
    return (request_of, request_of < lengths.shape[0], positions)


def partial_attention(grouped_queries, key_block, value_block, allowed):
    scores = jnp.einsum(
        "qkgd,nkd->kgqn", grouped_queries, key_block, preferred_element_type=jnp.float32
    ) / math.sqrt(grouped_queries.shape[-1])
    if allowed is not None:
        scores = jnp.where(allowed[None, None], scores, -jnp.inf)
    peak = jnp.max(scores, axis=-1)
    weights = jnp.exp(scores - peak[..., None])
    weight_sum = jnp.sum(weights, axis=-1)
    summed = jnp.einsum(
        "kgqn,nkd->kgqd",
        weights.astype(jnp.bfloat16),
        value_block,
        preferred_element_type=jnp.float32,
    )
    return (summed / weight_sum[..., None], peak + jnp.log(weight_sum))


def tile_of(size):
    return 256 if size % 256 == 0 else size


def over_tiles(size, body):
    tile = tile_of(size)
    if size == tile:
        body(pl.ds(0, tile))
        return

    @pl.loop(0, size // tile)
    def _(index):
        body(pl.ds(pl.multiple_of(index * tile, tile), tile))


def feed_forward_kernel(
    columns,
    normed_ref,
    residual_ref,
    live_ref,
    gate_hbm,
    up_hbm,
    down_hbm,
    out_ref,
    w_gate,
    w_up,
    w_down,
    rows,
    kept_sums,
    pair_out,
    pair_in,
    across_out,
    across_in,
    act,
    kept_down,
    term_out,
    term_in,
    sum_out,
    sum_in,
    total,
    weight_sems,
    send_sems,
    recv_sems,
):
    f32, bf16 = jnp.float32, jnp.bfloat16
    req, mlp = lax.axis_index("req"), lax.axis_index("mlp")
    column, pair = lax.div(req, 2), lax.rem(req, 2)
    high, low = lax.div(mlp, 2), lax.rem(mlp, 2)
    count = normed_ref.shape[0]
    part = count // 2
    width = normed_ref.shape[1]
    units = w_gate.shape[1]
    pair_peer = (column * 2 + 1 - pair, mlp)
    core_peer = (req, high * 2 + 1 - low)
    across_peer = (req, (1 - high) * 2 + low)

    def column_peer(shift):
        return (lax.rem(column + shift, columns) * 2 + pair, mlp)

    def copy(kind, k, src, dst, peer):
        return pltpu.make_async_remote_copy(
            src_ref=src,
            dst_ref=dst,
            send_sem=send_sems.at[kind, k],
            recv_sem=recv_sems.at[kind, k],
            device_id=peer,
            device_id_type=pl.DeviceIdType.MESH,
        )

    started = []

    def send(kind, k, src, dst, peer):
        descriptor = copy(kind, k, src, dst, peer)
        descriptor.start()
        started.append(descriptor)

    def receive(kind, k, dst, peer):
        copy(kind, k, dst, dst, peer).wait_recv()

    loads = [
        pltpu.make_async_copy(source, target, weight_sems.at[index])
        for index, (source, target) in enumerate(
            [(gate_hbm, w_gate), (up_hbm, w_up), (down_hbm, w_down)]
        )
    ]
    for load in loads:
        load.start()

    barrier = pltpu.get_barrier_semaphore()
    peers = [pair_peer, core_peer, across_peer] + [column_peer(k) for k in range(1, columns)]
    for peer in peers:
        pl.semaphore_signal(barrier, inc=1, device_id=peer, device_id_type=pl.DeviceIdType.MESH)
    pl.semaphore_wait(barrier, len(peers))

    send(1, 0, normed_ref, rows.at[0, pair], pair_peer)
    for k in range(1, columns):
        send(0, k, normed_ref, rows.at[k, pair], column_peer(columns - k))
    rows[0, pair] = normed_ref[...]

    def forward(k):
        receive(0, k, rows.at[k, pair], column_peer(k))
        send(1, k, rows.at[k, pair], rows.at[k, pair], pair_peer)

    def pick(value, which):
        return jnp.where(which == 0, value[:count], value[count:])

    def first_sums(k):
        receive(1, k, rows.at[k, 1 - pair], pair_peer)
        slot = k % 3
        for half, weight in enumerate((w_gate, w_up)):
            if k == 0:
                loads[half].wait()

            def body(at, half=half, weight=weight):
                sums = jnp.dot(
                    rows[k].reshape(2 * count, width), weight[:, at], preferred_element_type=f32
                )
                pair_out[k, half, :, at] = pick(sums, 1 - low).astype(bf16)
                kept_sums[slot, half, :, at] = pick(sums, low)

            over_tiles(units, body)
        send(2, k, pair_out.at[k], pair_in.at[k], core_peer)

    def second_sums(k):
        receive(2, k, pair_in.at[k], core_peer)
        at = pl.ds(pl.multiple_of((1 - high) * part, part), part)
        for half in range(2):
            across_out[k, half] = (
                kept_sums[k % 3, half, at, :] + pair_in[k, half, at, :].astype(f32)
            ).astype(bf16)
        send(3, k, across_out.at[k], across_in.at[k], across_peer)

    mine = low * count + high * part
    swapped = low * count + (1 - high) * part

    def act_rows(k, start):
        return act.at[k, pl.ds(pl.multiple_of(start, part), part), :]

    def activate(k):
        receive(3, k, across_in.at[k], across_peer)
        at = pl.ds(pl.multiple_of(high * part, part), part)
        gate, up = [
            kept_sums[k % 3, half, at, :]
            + pair_in[k, half, at, :].astype(f32)
            + across_in[k, half].astype(f32)
            for half in range(2)
        ]
        value = (gate / (1.0 + jnp.exp(-gate)) * up).astype(bf16)
        act[k, pl.ds(pl.multiple_of(mine, part), part), :] = value
        send(4, k, act_rows(k, mine), act_rows(k, mine), across_peer)
        send(5, k, act_rows(k, mine), act_rows(k, mine), core_peer)

    def down_terms(k):
        receive(4, k, act_rows(k, swapped), across_peer)
        send(6, k, act_rows(k, swapped), act_rows(k, swapped), core_peer)
        receive(5, k, act_rows(k, (1 - low) * count + high * part), core_peer)
        receive(6, k, act_rows(k, (1 - low) * count + (1 - high) * part), core_peer)
        if k == 0:
            loads[2].wait()

        def body(at):
            terms = jnp.dot(act[k], w_down[:, at], preferred_element_type=f32)
            term_out[k, :, at] = pick(terms, 1 - pair).astype(bf16)
            kept_down[k % 2, :, at] = pick(terms, pair)

        over_tiles(width, body)
        send(7, k, term_out.at[k], term_in.at[k], pair_peer)

    def pass_on(k):
        receive(7, k, term_in.at[k], pair_peer)
        value = kept_down[k % 2] + term_in[k].astype(f32)
        if k == 0:
            total[...] = value
            return
        sum_out[k] = value.astype(bf16)
        send(8, k, sum_out.at[k], sum_in.at[k], column_peer(k))

    for step in range(columns + 4):
        if step < columns:
            first_sums(step)
            second_sums(step)
            if step + 1 < columns:
                forward(step + 1)
        for behind, stage in ((1, activate), (2, down_terms), (3, pass_on)):
            if 0 <= step - behind < columns:
                stage(step - behind)
    down = total[...]
    for k in range(1, columns):
        receive(8, k, sum_in.at[k], column_peer(columns - k))
        down += sum_in[k].astype(f32)
    out_ref[...] = jnp.where(
        live_ref[...] > 0.0, residual_ref[...].astype(f32) + down, 0.0
    ).astype(bf16)
    for descriptor in started:
        descriptor.wait_send()


def feed_forward(normed_part, residual_part, live, w_gate, w_up, w_down):
    bf16, f32 = jnp.bfloat16, jnp.float32
    columns = lax.axis_size("req") // 2
    count, width = normed_part.shape
    units = w_gate.shape[1]
    in_vmem = pl.BlockSpec(memory_space=pltpu.VMEM)
    anywhere = pl.BlockSpec(memory_space=pl.ANY)
    return pl.pallas_call(
        functools.partial(feed_forward_kernel, columns),
        name="feed_forward",
        out_shape=jax.ShapeDtypeStruct((count, width), bf16),
        in_specs=[in_vmem] * 3 + [anywhere] * 3,
        out_specs=in_vmem,
        scratch_shapes=[
            pltpu.VMEM(w_gate.shape, bf16),
            pltpu.VMEM(w_up.shape, bf16),
            pltpu.VMEM(w_down.shape, bf16),
            pltpu.VMEM((columns, 2, count, width), bf16),
            pltpu.VMEM((3, 2, count, units), f32),
            pltpu.VMEM((columns, 2, count, units), bf16),
            pltpu.VMEM((columns, 2, count, units), bf16),
            pltpu.VMEM((columns, 2, count // 2, units), bf16),
            pltpu.VMEM((columns, 2, count // 2, units), bf16),
            pltpu.VMEM((columns, 2 * count, units), bf16),
            pltpu.VMEM((2, count, width), f32),
            pltpu.VMEM((columns, count, width), bf16),
            pltpu.VMEM((columns, count, width), bf16),
            pltpu.VMEM((columns, count, width), bf16),
            pltpu.VMEM((columns, count, width), bf16),
            pltpu.VMEM((count, width), f32),
            pltpu.SemaphoreType.DMA((3,)),
            pltpu.SemaphoreType.DMA((9, columns)),
            pltpu.SemaphoreType.DMA((9, columns)),
        ],
        compiler_params=pltpu.CompilerParams(
            collective_id=0, has_side_effects=True, vmem_limit_bytes=60 * 1024 * 1024
        ),
    )(normed_part, residual_part, live, w_gate, w_up, w_down)


def shards(
    hidden_in,
    attn_gain,
    w_query,
    w_key,
    w_value,
    w_out,
    mlp_gain,
    w_gate,
    w_up,
    w_down,
    prefix_kv,
    suffix_lengths,
    prefix_owner,
):
    f32 = jnp.float32
    bf16 = jnp.bfloat16
    slots_here = hidden_in.shape[0]
    width = hidden_in.shape[1]
    head_dim = HEAD_DIM
    kv_heads = w_key.shape[1] // head_dim
    q_heads = w_query.shape[1] // head_dim
    group = q_heads // kv_heads
    block_len = prefix_kv.shape[0]
    width_part = w_gate.shape[0]
    mlp_at = lax.axis_index("mlp")
    low, high = mlp_at % 2, mlp_at // 2
    width_start = mlp_at * width_part
    request_of, live, positions = slot_layout(suffix_lengths[0], slots_here)
    hidden_f = hidden_in.astype(f32)
    normed = rms_norm(hidden_f, attn_gain).astype(bf16)
    query_rows = rope(
        jnp.dot(normed, w_query, preferred_element_type=f32).reshape(
            slots_here, q_heads, head_dim
        ),
        positions,
    ).astype(bf16)
    all_queries = [query_rows] + [from_xor(query_rows, "req", mask) for mask in range(1, GSPAN)]
    key_rows = rope(
        jnp.dot(normed, w_key, preferred_element_type=f32).reshape(slots_here, kv_heads, head_dim),
        positions,
    ).astype(bf16)
    value_rows = (
        jnp.dot(normed, w_value, preferred_element_type=f32)
        .astype(bf16)
        .reshape(slots_here, kv_heads, head_dim)
    )
    place = lax.axis_index("req") % GSPAN
    group_id = lax.axis_index("req") // GSPAN
    owners = lax.dynamic_index_in_dim(prefix_owner, group_id, 0, keepdims=False)
    quarter = jnp.sum(jnp.where(owners == place, jnp.arange(GSPAN, dtype=jnp.int32), 0))
    prefix_pos = quarter * block_len + jnp.arange(block_len, dtype=jnp.int32)
    stored_keys = rope(
        prefix_kv[:, 0].reshape(block_len, kv_heads, head_dim).astype(f32), prefix_pos
    ).astype(bf16)
    stored_values = prefix_kv[:, 1].reshape(block_len, kv_heads, head_dim)
    slot_ids = jnp.arange(slots_here, dtype=jnp.int32)
    allowed = (request_of[:, None] == request_of[None, :]) & (
        slot_ids[None, :] <= slot_ids[:, None]
    )
    outs, tops = [], []
    for mask in range(GSPAN):
        grouped = all_queries[mask].reshape(slots_here, kv_heads, group, head_dim)
        out, top = partial_attention(grouped, stored_keys, stored_values, None)
        if mask:
            out = from_xor(out.astype(bf16), "req", mask).astype(f32)
            top = from_xor(top, "req", mask)
        outs.append(out)
        tops.append(top)
    out, top = partial_attention(
        query_rows.reshape(slots_here, kv_heads, group, head_dim), key_rows, value_rows, allowed
    )
    outs.append(out)
    tops.append(top)
    highest = tops[0]
    for top in tops[1:]:
        highest = jnp.maximum(highest, top)
    merged, total = 0.0, 0.0
    for out, top in zip(outs, tops):
        share = jnp.exp(top - highest)
        merged += out * share[..., None]
        total += share
    attended = (
        jnp.transpose(merged / total[..., None], (2, 0, 1, 3))
        .reshape(slots_here, q_heads * head_dim)
        .astype(bf16)
    )

    def term_part(index):
        start = index * width_part
        return jnp.dot(
            attended,
            lax.dynamic_slice_in_dim(w_out, start, width_part, 1),
            preferred_element_type=f32,
        )

    away, home = (1 - high) * 2, high * 2
    away_in = from_xor(term_part(away + 1 - low).astype(bf16), "mlp", 1)
    home_in = from_xor(term_part(home + 1 - low).astype(bf16), "mlp", 1)
    away_out = (term_part(away + low) + away_in.astype(f32)).astype(bf16)
    across = from_xor(away_out, "mlp", 2)
    head_total = term_part(home + low) + home_in.astype(f32) + across.astype(f32)
    hidden_part = lax.dynamic_slice_in_dim(hidden_in, width_start, width_part, 1)
    residual_part = (hidden_part.astype(f32) + head_total).astype(bf16)
    residual_f = residual_part.astype(f32)
    squares = jnp.sum(residual_f * residual_f, axis=-1)
    squares += from_xor(squares, "mlp", 1)
    squares += from_xor(squares, "mlp", 2)
    gain_part = lax.dynamic_slice_in_dim(mlp_gain, width_start, width_part, 0)
    normed_part = (
        residual_f * lax.rsqrt(squares / width + eps)[:, None] * gain_part.astype(f32)
    ).astype(bf16)

    hidden_out = feed_forward(
        normed_part, residual_part, live.astype(f32)[:, None], w_gate, w_up, w_down
    )
    stacked_kv = jnp.stack(
        [
            key_rows.reshape(slots_here, kv_heads * head_dim),
            value_rows.reshape(slots_here, kv_heads * head_dim),
        ],
        axis=1,
    )
    suffix_kv = jnp.where(live[:, None, None], stacked_kv, jnp.zeros_like(stacked_kv))
    return (hidden_out, suffix_kv)


def solution(mesh):
    placed = (
        P("req", None),
        P(),
        P(None, "mlp"),
        P(None, "mlp"),
        P(None, "mlp"),
        P("mlp", None),
        P(),
        P("mlp", "req"),
        P("mlp", "req"),
        P("req", "mlp"),
        P("req", None, "mlp"),
        P("req", None),
        P(),
    )
    return jax.shard_map(
        shards,
        mesh=mesh,
        in_specs=placed,
        out_specs=(P("req", "mlp"), P("req", None, "mlp")),
        check_vma=False,
    )
```

profile of v0, /device:TPU:13, one launch (start us, length us, event | category | flops | bytes accessed | tf_op | source)
XLA Modules:
  0.0 176.2 jit_solution(10824891489418256637)
XLA Ops:
  0.7 0.9 reduce-window.4
  1.6 0.7 fusion.108
  2.4 0.7 convert_element_type.156
  3.1 1.5 fusion.12
  4.7 3.4 %fusion.131 = f32[128,512]{1,0:T(8,128)S(1)} fusion(bf16[4096,512]{1,0:T(8,128)(2,1)} %param.15, bf16[128,4096]{1,0:T(8,128)(2,1)} %param.13, f32[4096]{0:T(1024)S(1)} %convert_element_type.156, f32[128]{0:T(128)S(1)} %add_rsqrt_fusion.1), kind=kOutput, calls=%fused_computation.167 | convolution fusion | flops 538968064 | bytes 5521920 | tf_op jit(solution)/shard_map/dot_general | solution.py:346
  8.3 0.3 multiply_cosine_fusion.1
  8.8 1.3 collective-permute-start
  10.3 1.3 collective-permute-start.4
  11.7 0.6 fusion.109
  13.0 1.5 fusion.133
  14.6 4.8 %fusion.70 = (bf16[2048,64]{1,0:T(8,128)(2,1)S(1)}, bf16[2048,64]{1,0:T(8,128)(2,1)S(1)}) fusion(f32[2048,1,128]{2,0,1:T(8,128)S(1)} %copy_convert_fusion, f32[64]{0:T(128)S(1)} %multiply_power_fusion, f32[2048]{0:T(1024)S(1)} %add_convert_fusion.3), kind=kLoop, calls=%fused_computation.84 | loop fusion | flops 1179648 | bytes 1581312 | tf_op jit(solution)/shard_map/concatenate | solution.py:33
  19.4 0.3 maximum_bitcast_fusion
  19.7 0.7 bitcast_reduce_fusion.3
  20.4 0.6 convolution_bitcast_fusion
  21.3 0.6 convolution_convert_fusion.2
  21.9 0.7 fusion.4
  22.9 1.9 %copy.70 = bf16[2048,1,128]{0,2,1:T(8,128)(2,1)} copy(bf16[2048,1,128]{2,1,0:T(2,128)(2,1)S(1)} %get-tuple-element.12) | data formatting | bytes 1048576
  24.8 1.7 bitcast_reduce_fusion.1
  26.5 0.7 fusion.9
  27.2 0.9 fusion.81
  28.1 1.6 bitcast_reduce_fusion.2
  29.7 0.7 fusion.7
  30.4 0.9 fusion.80
  31.6 0.7 bitcast_reduce_fusion
  32.3 0.7 fusion.11
  33.0 2.3 %collective-permute-start.5 = (f32[1,4,128]{2,1,0:T(4,128)S(1)}, f32[1,4,128]{2,1,0:T(4,128)S(1)}, u32[]{:S(2)}, u32[]{:S(2)}) collective-permute-start(f32[1,4,128]{2,1,0:T(4,128)S(1)} %add_bitcast_fusion.1), channel_id=1, source_target_pairs={{0,12},{4,8},{8,4},{12,0},{16,28},{20,24},{24,20},{28,16},{1,13},{... | collective-permute-start | bytes 6152 | tf_op jit(solution)/shard_map/ppermute | solution.py:22
  35.5 0.8 fusion.82
  36.4 1.3 collective-permute-start.6
  37.8 1.3 collective-permute-start.8
  39.4 0.9 collective-permute-done.6
  40.3 1.2 collective-permute-done.7
  41.5 1.5 collective-permute-done.8
  43.0 0.9 divide_convert_fusion
  43.9 1.6 convolution_convert_fusion
  45.5 3.8 %collective-permute-start.10 = (bf16[128,1024]{1,0:T(8,128)(2,1)S(1)}, bf16[128,1024]{1,0:T(8,128)(2,1)S(1)}, u32[]{:S(2)}, u32[]{:S(2)}) collective-permute-start(bf16[128,1024]{1,0:T(8,128)(2,1)S(1)} %convolution_convert_fusion), channel_id=1, source_target_pairs={{0,1},{1,0},{2,3},{3,2},{4,5},{5,4},{6,7},{7,6},{8,9},{9,8},{10,11... | collective-permute-start | bytes 786440 | tf_op jit(solution)/shard_map/ppermute | solution.py:22
  49.2 1.6 convolution_convert_fusion.1
  50.9 1.6 add_convert_fusion.1
  52.7 1.5 fusion.60
  54.3 5.6 %collective-permute-done.11 = bf16[128,1024]{1,0:T(8,128)(2,1)S(1)} collective-permute-done((bf16[128,1024]{1,0:T(8,128)(2,1)S(1)}, bf16[128,1024]{1,0:T(8,128)(2,1)S(1)}, u32[]{:S(2)}, u32[]{:S(2)}) %collective-permute-start.11) | collective-permute-done | bytes 262176 | tf_op jit(solution)/shard_map/ppermute | solution.py:22
  59.9 1.2 fusion.62
  61.1 1.4 collective-permute-start.12
  62.5 0.8 collective-permute-done.12
  63.5 0.7 dynamic-slice_convert_fusion
  64.2 0.7 copy.51.live_ref
  65.0 0.8 copy.52
  65.7 0.8 fusion.64.normed_ref
  66.6 108.0 %feed_forward.1 = bf16[128,1024]{1,0:T(8,128)(2,1)} custom-call(bf16[128,1024]{1,0:T(8,128)(2,1)} %fusion.64.normed_ref, bf16[128,1024]{1,0:T(8,128)(2,1)} %copy-done.4, f32[128,1]{1,0:T(8,128)} %copy.51.live_ref, bf16[1024,1792]{1,0:T(8,128)(2,1)} %gate_hbm.1, bf16[1024,1792]{1,0:T(8,128)(2,1)} %up_hbm.1, bf16[1792,1024]{1,0:T(8,128)(2,1)} %down_hbm.1), custom_call_target="tpu_custom_call" | custom-call | tf_op jit(solution)/shard_map/feed_forward/pallas_call | solution.py:281
  174.6 1.7 copy.80
  (59 shorter events, 3.1 us)
Async XLA Ops:
  0.6 19.8 %copy-start = (bf16[4096,128]{1,0:T(8,128)(2,1)S(1)}, bf16[4096,128]{1,0:T(8,128)(2,1)}, u32[]{:S(2)}) copy-start(bf16[4096,128]{1,0:T(8,128)(2,1)} %param.16) | copy-start | bytes 3145732
  4.6 7.0 %copy-start.7 = (s32[2,4]{1,0:T(2,128)S(1)}, s32[2,4]{1,0:T(2,128)}, u32[]{:S(2)}) copy-start(s32[2,4]{1,0:T(2,128)} %param.25) | copy-start | bytes 100
  4.6 8.3 %copy-start.3 = (bf16[2048,2,128]{2,1,0:T(2,128)(2,1)S(1)}, bf16[2048,2,128]{2,1,0:T(2,128)(2,1)}, u32[]{:S(2)}) copy-start(bf16[2048,2,128]{2,1,0:T(2,128)(2,1)} %param.23) | copy-start | bytes 3145732
  8.8 19.3 %collective-permute-start = (bf16[128,4,128]{2,0,1:T(8,128)(2,1)S(1)}, bf16[128,4,128]{2,0,1:T(8,128)(2,1)}, u32[]{:S(2)}, u32[]{:S(2)}) collective-permute-start(bf16[128,4,128]{2,0,1:T(8,128)(2,1)S(1)} %pad_maximum_fusion), channel_id=1, source_target_pairs={{0,4},{4,0},{8,12},{12,8},{16,20},{20,16},{24,28},{28,24},{1,5},{5... | collective-permute-start | bytes 393224 | tf_op jit(solution)/shard_map/ppermute | solution.py:22
  10.1 14.7 %collective-permute-start.2 = (bf16[128,4,128]{2,0,1:T(8,128)(2,1)S(1)}, bf16[128,4,128]{2,0,1:T(8,128)(2,1)}, u32[]{:S(2)}, u32[]{:S(2)}) collective-permute-start(bf16[128,4,128]{2,0,1:T(8,128)(2,1)S(1)} %pad_maximum_fusion), channel_id=1, source_target_pairs={{0,8},{4,12},{8,0},{12,4},{16,24},{20,28},{24,16},{28,20},{1,9},{5... | collective-permute-start | bytes 393224 | tf_op jit(solution)/shard_map/ppermute | solution.py:22
  10.3 21.3 %collective-permute-start.4 = (bf16[128,4,128]{2,0,1:T(8,128)(2,1)S(1)}, bf16[128,4,128]{2,0,1:T(8,128)(2,1)S(1)}, u32[]{:S(2)}, u32[]{:S(2)}) collective-permute-start(bf16[128,4,128]{2,0,1:T(8,128)(2,1)S(1)} %pad_maximum_fusion), channel_id=1, source_target_pairs={{0,12},{4,8},{8,4},{12,0},{16,28},{20,24},{24,20},{28,16},{1,13},{... | collective-permute-start | bytes 393224 | tf_op jit(solution)/shard_map/ppermute | solution.py:22
  14.6 5.9 %copy-start.5 = (bf16[128,4096]{1,0:T(8,128)(2,1)S(1)}, bf16[128,4096]{1,0:T(8,128)(2,1)}, u32[]{:S(2)}) copy-start(bf16[128,4096]{1,0:T(8,128)(2,1)} %param.13) | copy-start | bytes 3145732
  19.4 1.9 %copy-start.8 = (bf16[4096,128]{1,0:T(8,128)(2,1)S(1)}, bf16[4096,128]{1,0:T(8,128)(2,1)}, u32[]{:S(2)}) copy-start(bf16[4096,128]{1,0:T(8,128)(2,1)} %param.17) | copy-start | bytes 3145732
  20.4 2.2 %copy-start.1 = (f32[2048,128,4]{1,0,2:T(8,128)}, f32[2048,128,4]{1,0,2:T(8,128)S(1)}, u32[]{:S(2)}) copy-start(f32[2048,128,4]{1,0,2:T(8,128)S(1)} %get-tuple-element.32) | copy-start | bytes 12582916
  24.8 2.4 %copy-start.6 = (bf16[2048,1,128]{0,2,1:T(8,128)(2,1)S(1)}, bf16[2048,1,128]{0,2,1:T(8,128)(2,1)}, u32[]{:S(2)}) copy-start(bf16[2048,1,128]{0,2,1:T(8,128)(2,1)} %copy.70) | copy-start | bytes 1572868
  31.3 6.5 %collective-permute-start.3 = (f32[1,4,128]{2,1,0:T(4,128)S(1)}, f32[1,4,128]{2,1,0:T(4,128)S(1)}, u32[]{:S(2)}, u32[]{:S(2)}) collective-permute-start(f32[1,4,128]{2,1,0:T(4,128)S(1)} %add_bitcast_fusion.2), channel_id=1, source_target_pairs={{0,8},{4,12},{8,0},{12,4},{16,24},{20,28},{24,16},{28,20},{1,9},{5... | collective-permute-start | bytes 6152 | tf_op jit(solution)/shard_map/ppermute | solution.py:22
  33.0 10.0 %copy-start.2 = (f32[2048,128,4]{1,0,2:T(8,128)S(1)}, f32[2048,128,4]{1,0,2:T(8,128)}, u32[]{:S(2)}) copy-start(f32[2048,128,4]{1,0,2:T(8,128)} %copy-done.1) | copy-start | bytes 12582916
  33.0 6.1 %collective-permute-start.5 = (f32[1,4,128]{2,1,0:T(4,128)S(1)}, f32[1,4,128]{2,1,0:T(4,128)S(1)}, u32[]{:S(2)}, u32[]{:S(2)}) collective-permute-start(f32[1,4,128]{2,1,0:T(4,128)S(1)} %add_bitcast_fusion.1), channel_id=1, source_target_pairs={{0,12},{4,8},{8,4},{12,0},{16,28},{20,24},{24,20},{28,16},{1,13},{... | collective-permute-start | bytes 6152 | tf_op jit(solution)/shard_map/ppermute | solution.py:22
  35.3 3.8 %collective-permute-start.1 = (f32[1,4,128]{2,1,0:T(4,128)S(1)}, f32[1,4,128]{2,1,0:T(4,128)S(1)}, u32[]{:S(2)}, u32[]{:S(2)}) collective-permute-start(f32[1,4,128]{2,1,0:T(4,128)S(1)} %add_bitcast_fusion.3), channel_id=1, source_target_pairs={{0,4},{4,0},{8,12},{12,8},{16,20},{20,16},{24,28},{28,24},{1,5},{5... | collective-permute-start | bytes 6152 | tf_op jit(solution)/shard_map/ppermute | solution.py:22
  36.4 3.9 %collective-permute-start.6 = (bf16[1,4,128,128]{2,3,1,0:T(8,128)(2,1)S(1)}, bf16[1,4,128,128]{2,3,1,0:T(8,128)(2,1)S(1)}, u32[]{:S(2)}, u32[]{:S(2)}) collective-permute-start(bf16[1,4,128,128]{2,3,1,0:T(8,128)(2,1)S(1)} %fusion.80), channel_id=1, source_target_pairs={{0,4},{4,0},{8,12},{12,8},{16,20},{20,16},{24,28},{28,24},{1,5},{5... | collective-permute-start | bytes 393224 | tf_op jit(solution)/shard_map/ppermute | solution.py:22
  37.7 3.8 %collective-permute-start.7 = (bf16[1,4,128,128]{2,3,1,0:T(8,128)(2,1)S(1)}, bf16[1,4,128,128]{2,3,1,0:T(8,128)(2,1)S(1)}, u32[]{:S(2)}, u32[]{:S(2)}) collective-permute-start(bf16[1,4,128,128]{2,3,1,0:T(8,128)(2,1)S(1)} %fusion.81), channel_id=1, source_target_pairs={{0,8},{4,12},{8,0},{12,4},{16,24},{20,28},{24,16},{28,20},{1,9},{5... | collective-permute-start | bytes 393224 | tf_op jit(solution)/shard_map/ppermute | solution.py:22
  37.8 5.1 %collective-permute-start.8 = (bf16[1,4,128,128]{2,3,1,0:T(8,128)(2,1)S(1)}, bf16[1,4,128,128]{2,3,1,0:T(8,128)(2,1)S(1)}, u32[]{:S(2)}, u32[]{:S(2)}) collective-permute-start(bf16[1,4,128,128]{2,3,1,0:T(8,128)(2,1)S(1)} %fusion.82), channel_id=1, source_target_pairs={{0,12},{4,8},{8,4},{12,0},{16,28},{20,24},{24,20},{28,16},{1,13},{... | collective-permute-start | bytes 393224 | tf_op jit(solution)/shard_map/ppermute | solution.py:22
  45.5 5.4 %collective-permute-start.10 = (bf16[128,1024]{1,0:T(8,128)(2,1)S(1)}, bf16[128,1024]{1,0:T(8,128)(2,1)S(1)}, u32[]{:S(2)}, u32[]{:S(2)}) collective-permute-start(bf16[128,1024]{1,0:T(8,128)(2,1)S(1)} %convolution_convert_fusion), channel_id=1, source_target_pairs={{0,1},{1,0},{2,3},{3,2},{4,5},{5,4},{6,7},{7,6},{8,9},{9,8},{10,11... | collective-permute-start | bytes 786440 | tf_op jit(solution)/shard_map/ppermute | solution.py:22
  50.8 3.5 %collective-permute-start.9 = (bf16[128,1024]{1,0:T(8,128)(2,1)S(1)}, bf16[128,1024]{1,0:T(8,128)(2,1)S(1)}, u32[]{:S(2)}, u32[]{:S(2)}) collective-permute-start(bf16[128,1024]{1,0:T(8,128)(2,1)S(1)} %convolution_convert_fusion.1), channel_id=1, source_target_pairs={{0,1},{1,0},{2,3},{3,2},{4,5},{5,4},{6,7},{7,6},{8,9},{9,8},{10,11... | collective-permute-start | bytes 786440 | tf_op jit(solution)/shard_map/ppermute | solution.py:22
  52.4 7.5 %collective-permute-start.11 = (bf16[128,1024]{1,0:T(8,128)(2,1)S(1)}, bf16[128,1024]{1,0:T(8,128)(2,1)S(1)}, u32[]{:S(2)}, u32[]{:S(2)}) collective-permute-start(bf16[128,1024]{1,0:T(8,128)(2,1)S(1)} %add_convert_fusion.1), channel_id=1, source_target_pairs={{0,2},{1,3},{2,0},{3,1},{4,6},{5,7},{6,4},{7,5},{8,10},{9,11},{10,... | collective-permute-start | bytes 786440 | tf_op jit(solution)/shard_map/ppermute | solution.py:22
  61.1 5.5 %copy-start.4 = (bf16[128,1024]{1,0:T(8,128)(2,1)}, bf16[128,1024]{1,0:T(8,128)(2,1)S(1)}, u32[]{:S(2)}) copy-start(bf16[128,1024]{1,0:T(8,128)(2,1)S(1)} %get-tuple-element.7.residual_ref) | copy-start | bytes 786436
  61.1 2.2 %collective-permute-start.12 = (f32[128]{0:T(128)S(1)}, f32[128]{0:T(128)S(1)}, u32[]{:S(2)}, u32[]{:S(2)}) collective-permute-start(f32[128]{0:T(128)S(1)} %get-tuple-element.6), channel_id=1, source_target_pairs={{0,1},{1,0},{2,3},{3,2},{4,5},{5,4},{6,7},{7,6},{8,9},{9,8},{10,11... | collective-permute-start | bytes 1544 | tf_op jit(solution)/shard_map/ppermute | solution.py:22
  63.3 2.4 %collective-permute-start.13 = (f32[128]{0:T(128)S(1)}, f32[128]{0:T(128)S(1)}, u32[]{:S(2)}, u32[]{:S(2)}) collective-permute-start(f32[128]{0:T(128)S(1)} %add.240), channel_id=1, source_target_pairs={{0,2},{1,3},{2,0},{3,1},{4,6},{5,7},{6,4},{7,5},{8,10},{9,11},{10,... | collective-permute-start | bytes 1544 | tf_op jit(solution)/shard_map/ppermute | solution.py:22
where the time goes:
time: 179 us; the launch traced here: 176 us
  Pallas kernels  108 us (60%)
  matrix products  19.5 us (11%)
  other arithmetic  16.2 us (9%)
  starting transfers between devices  14 us (8%)
  waiting for transfers between devices  10 us (6%)
  local copies, waits for them, and re-layouts  6.86 us (4%)
    pallas_call x1, Pallas kernels, feed_forward(): pl.pallas_call(functools.partial(feed_forward_kernel, columns), name='fee...  108 us
    ppermute x14, starting transfers between devices, from_xor(): return lax.ppermute(value, axis, pairs)  14 us
    ppermute x14, waiting for transfers between devices, from_xor(): return lax.ppermute(value, axis, pairs)  10 us
    dot_general x4, matrix products, term_part(): jnp.dot(attended, lax.dynamic_slice_in_dim(w_out, start, width_part, 1),...  6.22 us
    concatenate x3, other arithmetic, rope(): jnp.concatenate([former * cosine - latter * sine, latter * cosine + forme...  5.22 us
    dot_general x5, matrix products, partial_attention(): jnp.einsum('qkgd,nkd->kgqn', grouped_queries, key_block, preferred_elemen...  4.95 us
    unnamed x21, local copies, waits for them, and re-layouts  4.33 us
    dot_general x5, matrix products, partial_attention(): jnp.einsum('kgqn,nkd->kgqd', weights.astype(jnp.bfloat16), value_block, p...  3.7 us
  transfers between devices with their start and end apart: 14, of which 5 were waited for; matrix products, arithmetic and copies ran while one was open for 16% of the time, Pallas kernels for 0%

commit v1 on v0

--- a/solution.py
+++ b/solution.py
@@ -3,6 +3,7 @@
 
 import jax
 import jax.numpy as jnp
+import numpy as np
 from jax import lax
 from jax.experimental import pallas as pl
 from jax.experimental.pallas import tpu as pltpu
@@ -33,6 +34,14 @@
     return jnp.concatenate(
         [former * cosine - latter * sine, latter * cosine + former * sine], axis=-1
     )
+
+
+def prefix_tables(head_dim):
+    half = head_dim // 2
+    exponents = -np.arange(half, dtype=np.float32) * np.float32(2.0) / np.float32(head_dim)
+    freq = np.power(np.float32(rope_base), exponents).astype(np.float32)
+    angle = np.arange(PREFIX, dtype=np.float32)[:, None] * freq[None, :]
+    return np.concatenate([np.cos(angle), np.sin(angle)], axis=1).astype(np.float32)
 
 
 def rms_norm(values, gain):
@@ -122,7 +131,9 @@
     req, mlp = lax.axis_index("req"), lax.axis_index("mlp")
     column, pair = lax.div(req, 2), lax.rem(req, 2)
     high, low = lax.div(mlp, 2), lax.rem(mlp, 2)
-    count = normed_ref.shape[0]
+    pieces = rows.shape[0] // columns
+    chunks = columns * pieces
+    count = normed_ref.shape[0] // pieces
     part = count // 2
     width = normed_ref.shape[1]
     units = w_gate.shape[1]
@@ -130,8 +141,15 @@
     core_peer = (req, high * 2 + 1 - low)
     across_peer = (req, (1 - high) * 2 + low)
 
-    def column_peer(shift):
-        return (lax.rem(column + shift, columns) * 2 + pair, mlp)
+    def column_peer(mask):
+        other = column
+        for bit in range(columns.bit_length() - 1):
+            if mask >> bit & 1:
+                other += (1 - 2 * lax.rem(lax.div(column, 1 << bit), 2)) * (1 << bit)
+        return (other * 2 + pair, mlp)
+
+    def piece(k):
+        return pl.ds(k % pieces * count, count)
 
     def copy(kind, k, src, dst, peer):
         return pltpu.make_async_remote_copy(
@@ -168,13 +186,15 @@
         pl.semaphore_signal(barrier, inc=1, device_id=peer, device_id_type=pl.DeviceIdType.MESH)
     pl.semaphore_wait(barrier, len(peers))
 
-    send(1, 0, normed_ref, rows.at[0, pair], pair_peer)
-    for k in range(1, columns):
-        send(0, k, normed_ref, rows.at[k, pair], column_peer(columns - k))
-    rows[0, pair] = normed_ref[...]
+    for k in range(chunks):
+        if k < pieces:
+            send(1, k, normed_ref.at[piece(k)], rows.at[k, pair], pair_peer)
+            rows[k, pair] = normed_ref[piece(k)]
+        else:
+            send(0, k, normed_ref.at[piece(k)], rows.at[k, pair], column_peer(k // pieces))
 
     def forward(k):
-        receive(0, k, rows.at[k, pair], column_peer(k))
+        receive(0, k, rows.at[k, pair], column_peer(k // pieces))
         send(1, k, rows.at[k, pair], rows.at[k, pair], pair_peer)
 
     def pick(value, which):
@@ -182,7 +202,7 @@
 
     def first_sums(k):
         receive(1, k, rows.at[k, 1 - pair], pair_peer)
-        slot = k % 3
+        slot = k % 4
         for half, weight in enumerate((w_gate, w_up)):
             if k == 0:
                 loads[half].wait()
@@ -202,7 +222,7 @@
         at = pl.ds(pl.multiple_of((1 - high) * part, part), part)
         for half in range(2):
             across_out[k, half] = (
-                kept_sums[k % 3, half, at, :] + pair_in[k, half, at, :].astype(f32)
+                kept_sums[k % 4, half, at, :] + pair_in[k, half, at, :].astype(f32)
             ).astype(bf16)
         send(3, k, across_out.at[k], across_in.at[k], across_peer)
 
@@ -216,7 +236,7 @@
         receive(3, k, across_in.at[k], across_peer)
         at = pl.ds(pl.multiple_of(high * part, part), part)
         gate, up = [
-            kept_sums[k % 3, half, at, :]
+            kept_sums[k % 4, half, at, :]
             + pair_in[k, half, at, :].astype(f32)
             + across_in[k, half].astype(f32)
             for half in range(2)
@@ -245,28 +265,30 @@
     def pass_on(k):
         receive(7, k, term_in.at[k], pair_peer)
         value = kept_down[k % 2] + term_in[k].astype(f32)
-        if k == 0:
-            total[...] = value
+        if k < pieces:
+            total[piece(k)] = value
             return
         sum_out[k] = value.astype(bf16)
-        send(8, k, sum_out.at[k], sum_in.at[k], column_peer(k))
-
-    for step in range(columns + 4):
-        if step < columns:
+        send(8, k, sum_out.at[k], sum_in.at[k], column_peer(k // pieces))
+
+    for step in range(chunks + 4):
+        if step < chunks:
             first_sums(step)
             second_sums(step)
-            if step + 1 < columns:
+            if pieces <= step + 1 < chunks:
                 forward(step + 1)
-        for behind, stage in ((1, activate), (2, down_terms), (3, pass_on)):
-            if 0 <= step - behind < columns:
+        for behind, stage in ((2, activate), (3, down_terms), (4, pass_on)):
+            if 0 <= step - behind < chunks:
                 stage(step - behind)
-    down = total[...]
-    for k in range(1, columns):
-        receive(8, k, sum_in.at[k], column_peer(columns - k))
-        down += sum_in[k].astype(f32)
-    out_ref[...] = jnp.where(
-        live_ref[...] > 0.0, residual_ref[...].astype(f32) + down, 0.0
-    ).astype(bf16)
+    for h in range(pieces):
+        at = piece(h)
+        down = total[at]
+        for k in range(h + pieces, chunks, pieces):
+            receive(8, k, sum_in.at[k], column_peer(k // pieces))
+            down += sum_in[k].astype(f32)
+        out_ref[at] = jnp.where(
+            live_ref[at] > 0.0, residual_ref[at].astype(f32) + down, 0.0
+        ).astype(bf16)
     for descriptor in started:
         descriptor.wait_send()
 
@@ -276,34 +298,38 @@
     columns = lax.axis_size("req") // 2
     count, width = normed_part.shape
     units = w_gate.shape[1]
+    total_rows = count
+    pieces = 2 if columns <= 4 else 1
+    chunks = columns * pieces
+    count = count // pieces
     in_vmem = pl.BlockSpec(memory_space=pltpu.VMEM)
     anywhere = pl.BlockSpec(memory_space=pl.ANY)
     return pl.pallas_call(
         functools.partial(feed_forward_kernel, columns),
         name="feed_forward",
-        out_shape=jax.ShapeDtypeStruct((count, width), bf16),
+        out_shape=jax.ShapeDtypeStruct((total_rows, width), bf16),
         in_specs=[in_vmem] * 3 + [anywhere] * 3,
         out_specs=in_vmem,
         scratch_shapes=[
             pltpu.VMEM(w_gate.shape, bf16),
             pltpu.VMEM(w_up.shape, bf16),
             pltpu.VMEM(w_down.shape, bf16),
-            pltpu.VMEM((columns, 2, count, width), bf16),
-            pltpu.VMEM((3, 2, count, units), f32),
-            pltpu.VMEM((columns, 2, count, units), bf16),
-            pltpu.VMEM((columns, 2, count, units), bf16),
-            pltpu.VMEM((columns, 2, count // 2, units), bf16),
-            pltpu.VMEM((columns, 2, count // 2, units), bf16),
-            pltpu.VMEM((columns, 2 * count, units), bf16),
+            pltpu.VMEM((chunks, 2, count, width), bf16),
+            pltpu.VMEM((4, 2, count, units), f32),
+            pltpu.VMEM((chunks, 2, count, units), bf16),
+            pltpu.VMEM((chunks, 2, count, units), bf16),
+            pltpu.VMEM((chunks, 2, count // 2, units), bf16),
+            pltpu.VMEM((chunks, 2, count // 2, units), bf16),
+            pltpu.VMEM((chunks, 2 * count, units), bf16),
             pltpu.VMEM((2, count, width), f32),
-            pltpu.VMEM((columns, count, width), bf16),
-            pltpu.VMEM((columns, count, width), bf16),
-            pltpu.VMEM((columns, count, width), bf16),
-            pltpu.VMEM((columns, count, width), bf16),
-            pltpu.VMEM((count, width), f32),
+            pltpu.VMEM((chunks, count, width), bf16),
+            pltpu.VMEM((chunks, count, width), bf16),
+            pltpu.VMEM((chunks, count, width), bf16),
+            pltpu.VMEM((chunks, count, width), bf16),
+            pltpu.VMEM((total_rows, width), f32),
             pltpu.SemaphoreType.DMA((3,)),
-            pltpu.SemaphoreType.DMA((9, columns)),
-            pltpu.SemaphoreType.DMA((9, columns)),
+            pltpu.SemaphoreType.DMA((9, chunks)),
+            pltpu.SemaphoreType.DMA((9, chunks)),
         ],
         compiler_params=pltpu.CompilerParams(
             collective_id=0, has_side_effects=True, vmem_limit_bytes=60 * 1024 * 1024
@@ -362,9 +388,14 @@
     group_id = lax.axis_index("req") // GSPAN
     owners = lax.dynamic_index_in_dim(prefix_owner, group_id, 0, keepdims=False)
     quarter = jnp.sum(jnp.where(owners == place, jnp.arange(GSPAN, dtype=jnp.int32), 0))
-    prefix_pos = quarter * block_len + jnp.arange(block_len, dtype=jnp.int32)
-    stored_keys = rope(
-        prefix_kv[:, 0].reshape(block_len, kv_heads, head_dim).astype(f32), prefix_pos
+    table = lax.dynamic_slice_in_dim(
+        jnp.asarray(prefix_tables(head_dim)), quarter * block_len, block_len, 0
+    )
+    cosine, sine = table[:, None, : head_dim // 2], table[:, None, head_dim // 2 :]
+    stored = prefix_kv[:, 0].reshape(block_len, kv_heads, head_dim).astype(f32)
+    former, latter = stored[..., : head_dim // 2], stored[..., head_dim // 2 :]
+    stored_keys = jnp.concatenate(
+        [former * cosine - latter * sine, latter * cosine + former * sine], axis=-1
     ).astype(bf16)
     stored_values = prefix_kv[:, 1].reshape(block_len, kv_heads, head_dim)
     slot_ids = jnp.arange(slots_here, dtype=jnp.int32)

time: 179 us -> 178 us (level); the launches traced: 176 us -> 178 us
  Pallas kernels: 108 us -> 112 us
  other arithmetic: 16.2 us -> 13.7 us
    concatenate x3 -> x1, other arithmetic: 5.22 us -> 0.11 us  [rope(): jnp.concatenate([former * cosine - latter * sine, latter * cosine + forme...]
    pallas_call x1, Pallas kernels: 108 us -> 112 us  [feed_forward(): pl.pallas_call(functools.partial(feed_forward_kernel, columns), name='fee...]
    concatenate x0 -> x2, other arithmetic: none -> 2.6 us  [shards(): jnp.concatenate([former * cosine - latter * sine, latter * cosine + forme...]
  transfers between devices with their start and end apart: 14 -> 14, of which waited for: 5 -> 5; matrix products, arithmetic and copies ran while one was open for 16% -> 14% of each run, Pallas kernels for 0% -> 0%
where the time goes in v1:
time: 178 us
  Pallas kernels  112 us (63%)
  matrix products  19.5 us (11%)
  starting transfers between devices  14 us (8%)
  other arithmetic  13.7 us (8%)
  waiting for transfers between devices  10 us (6%)
  local copies, waits for them, and re-layouts  7.03 us (4%)
    pallas_call x1, Pallas kernels, feed_forward(): pl.pallas_call(functools.partial(feed_forward_kernel, columns), name='fee...  112 us
    ppermute x14, starting transfers between devices, from_xor(): return lax.ppermute(value, axis, pairs)  14 us
    ppermute x14, waiting for transfers between devices, from_xor(): return lax.ppermute(value, axis, pairs)  10 us
    dot_general x4, matrix products, term_part(): jnp.dot(attended, lax.dynamic_slice_in_dim(w_out, start, width_part, 1),...  6.22 us
    dot_general x5, matrix products, partial_attention(): jnp.einsum('qkgd,nkd->kgqn', grouped_queries, key_block, preferred_elemen...  4.95 us
    unnamed x21, local copies, waits for them, and re-layouts  4.51 us
    dot_general x5, matrix products, partial_attention(): jnp.einsum('kgqn,nkd->kgqd', weights.astype(jnp.bfloat16), value_block, p...  3.7 us
  transfers between devices with their start and end apart: 14, of which 5 were waited for; matrix products, arithmetic and copies ran while one was open for 14% of the time, Pallas kernels for 0%

profile of v1, /device:TPU:13, one launch (start us, length us, event | category | flops | bytes accessed | tf_op | source)
XLA Modules:
  0.0 178.0 jit_solution(8096831093866713731)
XLA Ops:
  0.7 0.9 reduce-window.4
  1.6 0.7 fusion.108
  2.4 0.7 convert_element_type.148
  3.1 1.5 fusion.12
  4.7 3.4 %fusion.131 = f32[128,512]{1,0:T(8,128)S(1)} fusion(bf16[4096,512]{1,0:T(8,128)(2,1)} %param.16, bf16[128,4096]{1,0:T(8,128)(2,1)} %param.14, f32[4096]{0:T(1024)S(1)} %convert_element_type.148, f32[128]{0:T(128)S(1)} %add_rsqrt_fusion.1), kind=kOutput, calls=%fused_computation.166 | convolution fusion | flops 538968064 | bytes 5521920 | tf_op jit(solution)/shard_map/dot_general | solution.py:372
  8.3 0.3 multiply_cosine_fusion
  8.8 1.3 collective-permute-start
  10.3 1.3 collective-permute-start.4
  11.7 0.6 fusion.109
  13.0 1.5 fusion.133
  14.6 2.3 %fusion.70 = (bf16[2048,64]{1,0:T(8,128)(2,1)S(1)}, bf16[2048,64]{1,0:T(8,128)(2,1)S(1)}) fusion(f32[8192,128]{1,0:T(8,128)} %constant.102.clone, s32[]{:T(128)S(6)} %select_n.58, s32[]{:T(128)S(6)} %add.235, f32[2048,1,128]{2,0,1:T(8,128)S(1)} %copy_convert_fusion), kind=kLoop, calls=%fused_computation.84 | loop fusion | flops 1048576 | bytes 2621448 | tf_op jit(solution)/shard_map/concatenate | solution.py:397
  16.9 0.3 maximum_bitcast_fusion
  17.2 0.7 bitcast_reduce_fusion.3
  18.1 0.6 convolution_bitcast_fusion
  18.9 0.6 convolution_convert_fusion.2
  19.6 0.7 fusion.4
  20.5 1.9 %copy.71 = bf16[2048,1,128]{0,2,1:T(8,128)(2,1)} copy(bf16[2048,1,128]{2,1,0:T(2,128)(2,1)S(1)} %get-tuple-element.12) | data formatting | bytes 1048576
  22.4 1.7 bitcast_reduce_fusion.1
  24.1 0.7 fusion.9
  24.8 0.9 fusion.81
  25.7 1.6 bitcast_reduce_fusion.2
  27.4 0.7 fusion.7
  28.1 0.9 fusion.80
  29.1 0.7 bitcast_reduce_fusion
  29.8 0.7 fusion.11
  30.5 2.4 %collective-permute-start.5 = (f32[1,4,128]{2,1,0:T(4,128)S(1)}, f32[1,4,128]{2,1,0:T(4,128)S(1)}, u32[]{:S(2)}, u32[]{:S(2)}) collective-permute-start(f32[1,4,128]{2,1,0:T(4,128)S(1)} %add_bitcast_fusion.1), channel_id=1, source_target_pairs={{0,12},{4,8},{8,4},{12,0},{16,28},{20,24},{24,20},{28,16},{1,13},{... | collective-permute-start | bytes 6152 | tf_op jit(solution)/shard_map/ppermute | solution.py:23
  33.2 0.8 fusion.82
  34.0 1.3 collective-permute-start.6
  35.5 1.2 collective-permute-start.8
  37.0 0.9 collective-permute-done.6
  37.9 1.2 collective-permute-done.7
  39.2 1.4 collective-permute-done.8
  40.6 0.9 divide_convert_fusion
  41.5 1.6 convolution_convert_fusion
  43.1 3.8 %collective-permute-start.10 = (bf16[128,1024]{1,0:T(8,128)(2,1)S(1)}, bf16[128,1024]{1,0:T(8,128)(2,1)S(1)}, u32[]{:S(2)}, u32[]{:S(2)}) collective-permute-start(bf16[128,1024]{1,0:T(8,128)(2,1)S(1)} %convolution_convert_fusion), channel_id=1, source_target_pairs={{0,1},{1,0},{2,3},{3,2},{4,5},{5,4},{6,7},{7,6},{8,9},{9,8},{10,11... | collective-permute-start | bytes 786440 | tf_op jit(solution)/shard_map/ppermute | solution.py:23
  46.9 1.6 convolution_convert_fusion.1
  48.5 1.6 add_convert_fusion.1
  50.4 1.5 fusion.60
  51.9 5.6 %collective-permute-done.11 = bf16[128,1024]{1,0:T(8,128)(2,1)S(1)} collective-permute-done((bf16[128,1024]{1,0:T(8,128)(2,1)S(1)}, bf16[128,1024]{1,0:T(8,128)(2,1)S(1)}, u32[]{:S(2)}, u32[]{:S(2)}) %collective-permute-start.11) | collective-permute-done | bytes 262176 | tf_op jit(solution)/shard_map/ppermute | solution.py:23
  57.6 1.2 fusion.62
  58.8 1.4 collective-permute-start.12
  60.2 0.8 collective-permute-done.12
  61.2 0.7 dynamic-slice_convert_fusion
  61.9 0.7 copy.52.live_ref
  62.6 0.8 copy.53
  63.4 0.8 fusion.64.normed_ref
  64.2 112.1 %feed_forward.1 = bf16[128,1024]{1,0:T(8,128)(2,1)} custom-call(bf16[128,1024]{1,0:T(8,128)(2,1)} %fusion.64.normed_ref, bf16[128,1024]{1,0:T(8,128)(2,1)} %copy-done.4, f32[128,1]{1,0:T(8,128)} %copy.52.live_ref, bf16[1024,1792]{1,0:T(8,128)(2,1)} %gate_hbm.1, bf16[1024,1792]{1,0:T(8,128)(2,1)} %up_hbm.1, bf16[1792,1024]{1,0:T(8,128)(2,1)} %down_hbm.1), custom_call_target="tpu_custom_call" | custom-call | tf_op jit(solution)/shard_map/feed_forward/pallas_call | solution.py:307
  176.3 1.7 copy.81
  (58 shorter events, 3.2 us)
Async XLA Ops:
  0.6 17.3 %copy-start = (bf16[4096,128]{1,0:T(8,128)(2,1)S(1)}, bf16[4096,128]{1,0:T(8,128)(2,1)}, u32[]{:S(2)}) copy-start(bf16[4096,128]{1,0:T(8,128)(2,1)} %param.17) | copy-start | bytes 3145732
  4.6 7.0 %copy-start.7 = (s32[2,4]{1,0:T(2,128)S(1)}, s32[2,4]{1,0:T(2,128)}, u32[]{:S(2)}) copy-start(s32[2,4]{1,0:T(2,128)} %param.26) | copy-start | bytes 100
  4.6 8.3 %copy-start.3 = (bf16[2048,2,128]{2,1,0:T(2,128)(2,1)S(1)}, bf16[2048,2,128]{2,1,0:T(2,128)(2,1)}, u32[]{:S(2)}) copy-start(bf16[2048,2,128]{2,1,0:T(2,128)(2,1)} %param.24) | copy-start | bytes 3145732
  8.8 16.9 %collective-permute-start = (bf16[128,4,128]{2,0,1:T(8,128)(2,1)S(1)}, bf16[128,4,128]{2,0,1:T(8,128)(2,1)}, u32[]{:S(2)}, u32[]{:S(2)}) collective-permute-start(bf16[128,4,128]{2,0,1:T(8,128)(2,1)S(1)} %pad_maximum_fusion), channel_id=1, source_target_pairs={{0,4},{4,0},{8,12},{12,8},{16,20},{20,16},{24,28},{28,24},{1,5},{5... | collective-permute-start | bytes 393224 | tf_op jit(solution)/shard_map/ppermute | solution.py:23
  10.1 12.3 %collective-permute-start.2 = (bf16[128,4,128]{2,0,1:T(8,128)(2,1)S(1)}, bf16[128,4,128]{2,0,1:T(8,128)(2,1)}, u32[]{:S(2)}, u32[]{:S(2)}) collective-permute-start(bf16[128,4,128]{2,0,1:T(8,128)(2,1)S(1)} %pad_maximum_fusion), channel_id=1, source_target_pairs={{0,8},{4,12},{8,0},{12,4},{16,24},{20,28},{24,16},{28,20},{1,9},{5... | collective-permute-start | bytes 393224 | tf_op jit(solution)/shard_map/ppermute | solution.py:23
  10.3 18.8 %collective-permute-start.4 = (bf16[128,4,128]{2,0,1:T(8,128)(2,1)S(1)}, bf16[128,4,128]{2,0,1:T(8,128)(2,1)S(1)}, u32[]{:S(2)}, u32[]{:S(2)}) collective-permute-start(bf16[128,4,128]{2,0,1:T(8,128)(2,1)S(1)} %pad_maximum_fusion), channel_id=1, source_target_pairs={{0,12},{4,8},{8,4},{12,0},{16,28},{20,24},{24,20},{28,16},{1,13},{... | collective-permute-start | bytes 393224 | tf_op jit(solution)/shard_map/ppermute | solution.py:23
  16.9 1.2 copy-start.5
  16.9 2.1 %copy-start.8 = (bf16[4096,128]{1,0:T(8,128)(2,1)S(1)}, bf16[4096,128]{1,0:T(8,128)(2,1)}, u32[]{:S(2)}) copy-start(bf16[4096,128]{1,0:T(8,128)(2,1)} %param.18) | copy-start | bytes 3145732
  18.1 2.2 %copy-start.1 = (f32[2048,128,4]{1,0,2:T(8,128)}, f32[2048,128,4]{1,0,2:T(8,128)S(1)}, u32[]{:S(2)}) copy-start(f32[2048,128,4]{1,0,2:T(8,128)S(1)} %get-tuple-element.32) | copy-start | bytes 12582916
  22.4 2.4 %copy-start.6 = (bf16[2048,1,128]{0,2,1:T(8,128)(2,1)S(1)}, bf16[2048,1,128]{0,2,1:T(8,128)(2,1)}, u32[]{:S(2)}) copy-start(bf16[2048,1,128]{0,2,1:T(8,128)(2,1)} %copy.71) | copy-start | bytes 1572868
  28.9 6.6 %collective-permute-start.3 = (f32[1,4,128]{2,1,0:T(4,128)S(1)}, f32[1,4,128]{2,1,0:T(4,128)S(1)}, u32[]{:S(2)}, u32[]{:S(2)}) collective-permute-start(f32[1,4,128]{2,1,0:T(4,128)S(1)} %add_bitcast_fusion.2), channel_id=1, source_target_pairs={{0,8},{4,12},{8,0},{12,4},{16,24},{20,28},{24,16},{28,20},{1,9},{5... | collective-permute-start | bytes 6152 | tf_op jit(solution)/shard_map/ppermute | solution.py:23
  30.5 10.1 %copy-start.2 = (f32[2048,128,4]{1,0,2:T(8,128)S(1)}, f32[2048,128,4]{1,0,2:T(8,128)}, u32[]{:S(2)}) copy-start(f32[2048,128,4]{1,0,2:T(8,128)} %copy-done.1) | copy-start | bytes 12582916
  30.5 6.2 %collective-permute-start.5 = (f32[1,4,128]{2,1,0:T(4,128)S(1)}, f32[1,4,128]{2,1,0:T(4,128)S(1)}, u32[]{:S(2)}, u32[]{:S(2)}) collective-permute-start(f32[1,4,128]{2,1,0:T(4,128)S(1)} %add_bitcast_fusion.1), channel_id=1, source_target_pairs={{0,12},{4,8},{8,4},{12,0},{16,28},{20,24},{24,20},{28,16},{1,13},{... | collective-permute-start | bytes 6152 | tf_op jit(solution)/shard_map/ppermute | solution.py:23
  33.0 3.8 %collective-permute-start.1 = (f32[1,4,128]{2,1,0:T(4,128)S(1)}, f32[1,4,128]{2,1,0:T(4,128)S(1)}, u32[]{:S(2)}, u32[]{:S(2)}) collective-permute-start(f32[1,4,128]{2,1,0:T(4,128)S(1)} %add_bitcast_fusion.3), channel_id=1, source_target_pairs={{0,4},{4,0},{8,12},{12,8},{16,20},{20,16},{24,28},{28,24},{1,5},{5... | collective-permute-start | bytes 6152 | tf_op jit(solution)/shard_map/ppermute | solution.py:23
  34.0 3.9 %collective-permute-start.6 = (bf16[1,4,128,128]{2,3,1,0:T(8,128)(2,1)S(1)}, bf16[1,4,128,128]{2,3,1,0:T(8,128)(2,1)S(1)}, u32[]{:S(2)}, u32[]{:S(2)}) collective-permute-start(bf16[1,4,128,128]{2,3,1,0:T(8,128)(2,1)S(1)} %fusion.80), channel_id=1, source_target_pairs={{0,4},{4,0},{8,12},{12,8},{16,20},{20,16},{24,28},{28,24},{1,5},{5... | collective-permute-start | bytes 393224 | tf_op jit(solution)/shard_map/ppermute | solution.py:23
  35.3 3.8 %collective-permute-start.7 = (bf16[1,4,128,128]{2,3,1,0:T(8,128)(2,1)S(1)}, bf16[1,4,128,128]{2,3,1,0:T(8,128)(2,1)S(1)}, u32[]{:S(2)}, u32[]{:S(2)}) collective-permute-start(bf16[1,4,128,128]{2,3,1,0:T(8,128)(2,1)S(1)} %fusion.81), channel_id=1, source_target_pairs={{0,8},{4,12},{8,0},{12,4},{16,24},{20,28},{24,16},{28,20},{1,9},{5... | collective-permute-start | bytes 393224 | tf_op jit(solution)/shard_map/ppermute | solution.py:23
  35.5 5.1 %collective-permute-start.8 = (bf16[1,4,128,128]{2,3,1,0:T(8,128)(2,1)S(1)}, bf16[1,4,128,128]{2,3,1,0:T(8,128)(2,1)S(1)}, u32[]{:S(2)}, u32[]{:S(2)}) collective-permute-start(bf16[1,4,128,128]{2,3,1,0:T(8,128)(2,1)S(1)} %fusion.82), channel_id=1, source_target_pairs={{0,12},{4,8},{8,4},{12,0},{16,28},{20,24},{24,20},{28,16},{1,13},{... | collective-permute-start | bytes 393224 | tf_op jit(solution)/shard_map/ppermute | solution.py:23
  43.1 5.4 %collective-permute-start.10 = (bf16[128,1024]{1,0:T(8,128)(2,1)S(1)}, bf16[128,1024]{1,0:T(8,128)(2,1)S(1)}, u32[]{:S(2)}, u32[]{:S(2)}) collective-permute-start(bf16[128,1024]{1,0:T(8,128)(2,1)S(1)} %convolution_convert_fusion), channel_id=1, source_target_pairs={{0,1},{1,0},{2,3},{3,2},{4,5},{5,4},{6,7},{7,6},{8,9},{9,8},{10,11... | collective-permute-start | bytes 786440 | tf_op jit(solution)/shard_map/ppermute | solution.py:23
  48.4 3.5 %collective-permute-start.9 = (bf16[128,1024]{1,0:T(8,128)(2,1)S(1)}, bf16[128,1024]{1,0:T(8,128)(2,1)S(1)}, u32[]{:S(2)}, u32[]{:S(2)}) collective-permute-start(bf16[128,1024]{1,0:T(8,128)(2,1)S(1)} %convolution_convert_fusion.1), channel_id=1, source_target_pairs={{0,1},{1,0},{2,3},{3,2},{4,5},{5,4},{6,7},{7,6},{8,9},{9,8},{10,11... | collective-permute-start | bytes 786440 | tf_op jit(solution)/shard_map/ppermute | solution.py:23
  50.1 7.5 %collective-permute-start.11 = (bf16[128,1024]{1,0:T(8,128)(2,1)S(1)}, bf16[128,1024]{1,0:T(8,128)(2,1)S(1)}, u32[]{:S(2)}, u32[]{:S(2)}) collective-permute-start(bf16[128,1024]{1,0:T(8,128)(2,1)S(1)} %add_convert_fusion.1), channel_id=1, source_target_pairs={{0,2},{1,3},{2,0},{3,1},{4,6},{5,7},{6,4},{7,5},{8,10},{9,11},{10,... | collective-permute-start | bytes 786440 | tf_op jit(solution)/shard_map/ppermute | solution.py:23
  58.8 5.5 %copy-start.4 = (bf16[128,1024]{1,0:T(8,128)(2,1)}, bf16[128,1024]{1,0:T(8,128)(2,1)S(1)}, u32[]{:S(2)}) copy-start(bf16[128,1024]{1,0:T(8,128)(2,1)S(1)} %get-tuple-element.7.residual_ref) | copy-start | bytes 786436
  58.8 2.2 %collective-permute-start.12 = (f32[128]{0:T(128)S(1)}, f32[128]{0:T(128)S(1)}, u32[]{:S(2)}, u32[]{:S(2)}) collective-permute-start(f32[128]{0:T(128)S(1)} %get-tuple-element.6), channel_id=1, source_target_pairs={{0,1},{1,0},{2,3},{3,2},{4,5},{5,4},{6,7},{7,6},{8,9},{9,8},{10,11... | collective-permute-start | bytes 1544 | tf_op jit(solution)/shard_map/ppermute | solution.py:23
  61.0 2.4 %collective-permute-start.13 = (f32[128]{0:T(128)S(1)}, f32[128]{0:T(128)S(1)}, u32[]{:S(2)}, u32[]{:S(2)}) collective-permute-start(f32[128]{0:T(128)S(1)} %add.232), channel_id=1, source_target_pairs={{0,2},{1,3},{2,0},{3,1},{4,6},{5,7},{6,4},{7,5},{8,10},{9,11},{10,... | collective-permute-start | bytes 1544 | tf_op jit(solution)/shard_map/ppermute | solution.py:23

commit v2 on v1

--- a/solution.py
+++ b/solution.py
@@ -271,13 +271,16 @@
         sum_out[k] = value.astype(bf16)
         send(8, k, sum_out.at[k], sum_in.at[k], column_peer(k // pieces))
 
-    for step in range(chunks + 4):
+    for step in range(chunks + 5):
         if step < chunks:
             first_sums(step)
+        if pieces <= step - 1 < chunks or 0 <= step - 1 < pieces - 1:
+            second_sums(step - 1)
+        if step == pieces - 1:
             second_sums(step)
-            if pieces <= step + 1 < chunks:
-                forward(step + 1)
-        for behind, stage in ((2, activate), (3, down_terms), (4, pass_on)):
+        if pieces <= step + 1 < chunks:
+            forward(step + 1)
+        for behind, stage in ((3, activate), (4, down_terms), (5, pass_on)):
             if 0 <= step - behind < chunks:
                 stage(step - behind)
     for h in range(pieces):
@@ -430,13 +433,10 @@
         .astype(bf16)
     )
 
+    head_terms = jnp.dot(attended, w_out, preferred_element_type=f32)
+
     def term_part(index):
-        start = index * width_part
-        return jnp.dot(
-            attended,
-            lax.dynamic_slice_in_dim(w_out, start, width_part, 1),
-            preferred_element_type=f32,
-        )
+        return lax.dynamic_slice_in_dim(head_terms, index * width_part, width_part, 1)
 
     away, home = (1 - high) * 2, high * 2
     away_in = from_xor(term_part(away + 1 - low).astype(bf16), "mlp", 1)

time: 178 us -> 177 us (level)
  matrix products: 19.5 us -> 14.1 us
  waiting for transfers between devices: 10 us -> 13.9 us
  Pallas kernels: 112 us -> 110 us
  other arithmetic: 13.7 us -> 15.6 us
    dot_general x4 -> x1, matrix products: 6.22 us -> 0.75 us  [shards(): head_terms = jnp.dot(attended, w_out, preferred_element_type=f32)]
    ppermute x14, waiting for transfers between devices: 10 us -> 13.9 us  [from_xor(): return lax.ppermute(value, axis, pairs)]
    pallas_call x1, Pallas kernels: 112 us -> 110 us  [feed_forward(): pl.pallas_call(functools.partial(feed_forward_kernel, columns), name='fee...]
    unnamed x21 -> x23, local copies, waits for them, and re-layouts: 4.51 us -> 4.52 us
  transfers between devices with their start and end apart: 14 -> 14, of which waited for: 5 -> 6; matrix products, arithmetic and copies ran while one was open for 14% -> 13% of each run, Pallas kernels for 0% -> 0%
where the time goes in v2:
time: 177 us; the launch traced here: 176 us
  Pallas kernels  110 us (62%)
  other arithmetic  15.6 us (9%)
  matrix products  14.1 us (8%)
  waiting for transfers between devices  13.9 us (8%)
  starting transfers between devices  13.6 us (8%)
  local copies, waits for them, and re-layouts  7.83 us (4%)
    pallas_call x1, Pallas kernels, feed_forward(): pl.pallas_call(functools.partial(feed_forward_kernel, columns), name='fee...  110 us
    ppermute x14, waiting for transfers between devices, from_xor(): return lax.ppermute(value, axis, pairs)  13.9 us
    ppermute x14, starting transfers between devices, from_xor(): return lax.ppermute(value, axis, pairs)  13.6 us
    dot_general x5, matrix products, partial_attention(): jnp.einsum('qkgd,nkd->kgqn', grouped_queries, key_block, preferred_elemen...  4.95 us
    unnamed x23, local copies, waits for them, and re-layouts  4.52 us
    dot_general x5, matrix products, partial_attention(): jnp.einsum('kgqn,nkd->kgqd', weights.astype(jnp.bfloat16), value_block, p...  3.72 us
  transfers between devices with their start and end apart: 14, of which 6 were waited for; matrix products, arithmetic and copies ran while one was open for 13% of the time, Pallas kernels for 0%

profile of v2, /device:TPU:13, one launch (start us, length us, event | category | flops | bytes accessed | tf_op | source)
XLA Modules:
  0.0 176.4 jit_solution(15560929775054941734)
XLA Ops:
  0.7 0.9 reduce-window.4
  1.6 0.7 fusion.96
  2.4 0.7 convert_element_type.148
  3.1 1.5 fusion.12
  4.7 3.4 %fusion.119 = f32[128,512]{1,0:T(8,128)S(1)} fusion(bf16[4096,512]{1,0:T(8,128)(2,1)} %param.16, bf16[128,4096]{1,0:T(8,128)(2,1)} %param.14, f32[4096]{0:T(1024)S(1)} %convert_element_type.148, f32[128]{0:T(128)S(1)} %add_rsqrt_fusion.1), kind=kOutput, calls=%fused_computation.156 | convolution fusion | flops 538968064 | bytes 5521920 | tf_op jit(solution)/shard_map/dot_general | solution.py:375
  8.3 0.3 multiply_cosine_fusion
  8.8 1.3 collective-permute-start
  10.3 1.3 collective-permute-start.4
  11.7 0.6 fusion.97
  13.0 1.5 fusion.121
  14.6 2.3 %fusion.64 = (bf16[2048,64]{1,0:T(8,128)(2,1)S(1)}, bf16[2048,64]{1,0:T(8,128)(2,1)S(1)}) fusion(f32[8192,128]{1,0:T(8,128)} %constant.102.clone, s32[]{:T(128)S(6)} %select_n.58, s32[]{:T(128)S(6)} %add.235, f32[2048,1,128]{2,0,1:T(8,128)S(1)} %copy_convert_fusion), kind=kLoop, calls=%fused_computation.78 | loop fusion | flops 1048576 | bytes 2621448 | tf_op jit(solution)/shard_map/concatenate | solution.py:400
  16.9 0.3 maximum_bitcast_fusion
  17.2 0.7 bitcast_reduce_fusion.3
  18.1 0.6 convolution_bitcast_fusion
  18.9 0.6 convolution_convert_fusion
  19.6 0.7 fusion.4
  20.6 1.9 %copy.71 = bf16[2048,1,128]{0,2,1:T(8,128)(2,1)} copy(bf16[2048,1,128]{2,1,0:T(2,128)(2,1)S(1)} %get-tuple-element.14) | data formatting | bytes 1048576
  22.5 1.7 bitcast_reduce_fusion.1
  24.2 0.7 fusion.9
  24.9 0.9 fusion.75
  25.8 1.6 bitcast_reduce_fusion.2
  27.4 0.7 fusion.7
  28.1 0.9 fusion.74
  29.2 0.7 bitcast_reduce_fusion
  29.9 0.7 fusion.11
  30.6 2.4 %collective-permute-start.5 = (f32[1,4,128]{2,1,0:T(4,128)S(1)}, f32[1,4,128]{2,1,0:T(4,128)S(1)}, u32[]{:S(2)}, u32[]{:S(2)}) collective-permute-start(f32[1,4,128]{2,1,0:T(4,128)S(1)} %add_bitcast_fusion.1), channel_id=1, source_target_pairs={{0,12},{4,8},{8,4},{12,0},{16,28},{20,24},{24,20},{28,16},{1,13},{... | collective-permute-start | bytes 6152 | tf_op jit(solution)/shard_map/ppermute | solution.py:23
  33.2 0.9 fusion.76
  34.1 1.3 collective-permute-start.6
  35.6 1.3 collective-permute-start.8
  37.1 0.9 collective-permute-done.6
  38.0 1.2 collective-permute-done.7
  39.2 1.4 collective-permute-done.8
  40.7 0.9 divide_convert_fusion
  41.6 0.8 fusion.124
  42.4 0.8 dynamic-slice_convert_fusion.1
  43.2 3.7 %collective-permute-start.10 = (bf16[128,1024]{1,0:T(8,128)(2,1)}, bf16[128,1024]{1,0:T(8,128)(2,1)}, u32[]{:S(2)}, u32[]{:S(2)}) collective-permute-start(bf16[128,1024]{1,0:T(8,128)(2,1)} %get-tuple-element.13), channel_id=1, source_target_pairs={{0,1},{1,0},{2,3},{3,2},{4,5},{5,4},{6,7},{7,6},{8,9},{9,8},{10,11... | collective-permute-start | bytes 786440 | tf_op jit(solution)/shard_map/ppermute | solution.py:23
  46.9 1.8 %collective-permute-done.10 = bf16[128,1024]{1,0:T(8,128)(2,1)} collective-permute-done((bf16[128,1024]{1,0:T(8,128)(2,1)}, bf16[128,1024]{1,0:T(8,128)(2,1)}, u32[]{:S(2)}, u32[]{:S(2)}) %collective-permute-start.10) | collective-permute-done | bytes 262176 | tf_op jit(solution)/shard_map/ppermute | solution.py:23
  48.7 1.7 add_convert_fusion.1
  50.6 7.6 %collective-permute-done.11 = bf16[128,1024]{1,0:T(8,128)(2,1)} collective-permute-done((bf16[128,1024]{1,0:T(8,128)(2,1)}, bf16[128,1024]{1,0:T(8,128)(2,1)}, u32[]{:S(2)}, u32[]{:S(2)}) %collective-permute-start.11) | collective-permute-done | bytes 262176 | tf_op jit(solution)/shard_map/ppermute | solution.py:23
  58.2 1.3 fusion.56
  59.6 1.3 collective-permute-start.12
  60.9 0.8 collective-permute-done.12
  61.9 0.7 dynamic-slice_convert_fusion.2
  62.6 0.7 copy.52.live_ref
  63.3 0.8 copy.53
  64.1 0.8 fusion.58.normed_ref
  64.9 109.8 %feed_forward.1 = bf16[128,1024]{1,0:T(8,128)(2,1)} custom-call(bf16[128,1024]{1,0:T(8,128)(2,1)} %fusion.58.normed_ref, bf16[128,1024]{1,0:T(8,128)(2,1)} %copy-done.5, f32[128,1]{1,0:T(8,128)} %copy.52.live_ref, bf16[1024,1792]{1,0:T(8,128)(2,1)} %gate_hbm.1, bf16[1024,1792]{1,0:T(8,128)(2,1)} %up_hbm.1, bf16[1792,1024]{1,0:T(8,128)(2,1)} %down_hbm.1), custom_call_target="tpu_custom_call" | custom-call | tf_op jit(solution)/shard_map/feed_forward/pallas_call | solution.py:310
  174.7 1.7 copy.81
  (59 shorter events, 3.0 us)
Async XLA Ops:
  0.6 17.3 %copy-start = (bf16[4096,128]{1,0:T(8,128)(2,1)S(1)}, bf16[4096,128]{1,0:T(8,128)(2,1)}, u32[]{:S(2)}) copy-start(bf16[4096,128]{1,0:T(8,128)(2,1)} %param.17) | copy-start | bytes 3145732
  4.6 7.0 %copy-start.8 = (s32[2,4]{1,0:T(2,128)S(1)}, s32[2,4]{1,0:T(2,128)}, u32[]{:S(2)}) copy-start(s32[2,4]{1,0:T(2,128)} %param.26) | copy-start | bytes 100
  4.6 8.3 %copy-start.4 = (bf16[2048,2,128]{2,1,0:T(2,128)(2,1)S(1)}, bf16[2048,2,128]{2,1,0:T(2,128)(2,1)}, u32[]{:S(2)}) copy-start(bf16[2048,2,128]{2,1,0:T(2,128)(2,1)} %param.24) | copy-start | bytes 3145732
  8.8 17.0 %collective-permute-start = (bf16[128,4,128]{2,0,1:T(8,128)(2,1)S(1)}, bf16[128,4,128]{2,0,1:T(8,128)(2,1)}, u32[]{:S(2)}, u32[]{:S(2)}) collective-permute-start(bf16[128,4,128]{2,0,1:T(8,128)(2,1)S(1)} %pad_maximum_fusion), channel_id=1, source_target_pairs={{0,4},{4,0},{8,12},{12,8},{16,20},{20,16},{24,28},{28,24},{1,5},{5... | collective-permute-start | bytes 393224 | tf_op jit(solution)/shard_map/ppermute | solution.py:23
  10.1 12.4 %collective-permute-start.2 = (bf16[128,4,128]{2,0,1:T(8,128)(2,1)S(1)}, bf16[128,4,128]{2,0,1:T(8,128)(2,1)}, u32[]{:S(2)}, u32[]{:S(2)}) collective-permute-start(bf16[128,4,128]{2,0,1:T(8,128)(2,1)S(1)} %pad_maximum_fusion), channel_id=1, source_target_pairs={{0,8},{4,12},{8,0},{12,4},{16,24},{20,28},{24,16},{28,20},{1,9},{5... | collective-permute-start | bytes 393224 | tf_op jit(solution)/shard_map/ppermute | solution.py:23
  10.3 18.9 %collective-permute-start.4 = (bf16[128,4,128]{2,0,1:T(8,128)(2,1)S(1)}, bf16[128,4,128]{2,0,1:T(8,128)(2,1)S(1)}, u32[]{:S(2)}, u32[]{:S(2)}) collective-permute-start(bf16[128,4,128]{2,0,1:T(8,128)(2,1)S(1)} %pad_maximum_fusion), channel_id=1, source_target_pairs={{0,12},{4,8},{8,4},{12,0},{16,28},{20,24},{24,20},{28,16},{1,13},{... | collective-permute-start | bytes 393224 | tf_op jit(solution)/shard_map/ppermute | solution.py:23
  16.9 1.2 copy-start.6
  16.9 2.1 %copy-start.9 = (bf16[4096,128]{1,0:T(8,128)(2,1)S(1)}, bf16[4096,128]{1,0:T(8,128)(2,1)}, u32[]{:S(2)}) copy-start(bf16[4096,128]{1,0:T(8,128)(2,1)} %param.18) | copy-start | bytes 3145732
  18.1 2.2 %copy-start.1 = (f32[2048,128,4]{1,0,2:T(8,128)}, f32[2048,128,4]{1,0,2:T(8,128)S(1)}, u32[]{:S(2)}) copy-start(f32[2048,128,4]{1,0,2:T(8,128)S(1)} %get-tuple-element.34) | copy-start | bytes 12582916
  22.5 2.4 %copy-start.7 = (bf16[2048,1,128]{0,2,1:T(8,128)(2,1)S(1)}, bf16[2048,1,128]{0,2,1:T(8,128)(2,1)}, u32[]{:S(2)}) copy-start(bf16[2048,1,128]{0,2,1:T(8,128)(2,1)} %copy.71) | copy-start | bytes 1572868
  29.0 6.6 %collective-permute-start.3 = (f32[1,4,128]{2,1,0:T(4,128)S(1)}, f32[1,4,128]{2,1,0:T(4,128)S(1)}, u32[]{:S(2)}, u32[]{:S(2)}) collective-permute-start(f32[1,4,128]{2,1,0:T(4,128)S(1)} %add_bitcast_fusion.2), channel_id=1, source_target_pairs={{0,8},{4,12},{8,0},{12,4},{16,24},{20,28},{24,16},{28,20},{1,9},{5... | collective-permute-start | bytes 6152 | tf_op jit(solution)/shard_map/ppermute | solution.py:23
  30.6 10.1 %copy-start.2 = (f32[2048,128,4]{1,0,2:T(8,128)S(1)}, f32[2048,128,4]{1,0,2:T(8,128)}, u32[]{:S(2)}) copy-start(f32[2048,128,4]{1,0,2:T(8,128)} %copy-done.1) | copy-start | bytes 12582916
  30.6 6.2 %collective-permute-start.5 = (f32[1,4,128]{2,1,0:T(4,128)S(1)}, f32[1,4,128]{2,1,0:T(4,128)S(1)}, u32[]{:S(2)}, u32[]{:S(2)}) collective-permute-start(f32[1,4,128]{2,1,0:T(4,128)S(1)} %add_bitcast_fusion.1), channel_id=1, source_target_pairs={{0,12},{4,8},{8,4},{12,0},{16,28},{20,24},{24,20},{28,16},{1,13},{... | collective-permute-start | bytes 6152 | tf_op jit(solution)/shard_map/ppermute | solution.py:23
  33.0 3.8 %collective-permute-start.1 = (f32[1,4,128]{2,1,0:T(4,128)S(1)}, f32[1,4,128]{2,1,0:T(4,128)S(1)}, u32[]{:S(2)}, u32[]{:S(2)}) collective-permute-start(f32[1,4,128]{2,1,0:T(4,128)S(1)} %add_bitcast_fusion.3), channel_id=1, source_target_pairs={{0,4},{4,0},{8,12},{12,8},{16,20},{20,16},{24,28},{28,24},{1,5},{5... | collective-permute-start | bytes 6152 | tf_op jit(solution)/shard_map/ppermute | solution.py:23
  34.1 7.5 %copy-start.3 = (bf16[512,4096]{1,0:T(8,128)(2,1)S(1)}, bf16[512,4096]{1,0:T(8,128)(2,1)}, u32[]{:S(2)}) copy-start(bf16[512,4096]{1,0:T(8,128)(2,1)} %param.19) | copy-start | bytes 12582916
  34.1 3.9 %collective-permute-start.6 = (bf16[1,4,128,128]{2,3,1,0:T(8,128)(2,1)S(1)}, bf16[1,4,128,128]{2,3,1,0:T(8,128)(2,1)S(1)}, u32[]{:S(2)}, u32[]{:S(2)}) collective-permute-start(bf16[1,4,128,128]{2,3,1,0:T(8,128)(2,1)S(1)} %fusion.74), channel_id=1, source_target_pairs={{0,4},{4,0},{8,12},{12,8},{16,20},{20,16},{24,28},{28,24},{1,5},{5... | collective-permute-start | bytes 393224 | tf_op jit(solution)/shard_map/ppermute | solution.py:23
  35.4 3.8 %collective-permute-start.7 = (bf16[1,4,128,128]{2,3,1,0:T(8,128)(2,1)S(1)}, bf16[1,4,128,128]{2,3,1,0:T(8,128)(2,1)S(1)}, u32[]{:S(2)}, u32[]{:S(2)}) collective-permute-start(bf16[1,4,128,128]{2,3,1,0:T(8,128)(2,1)S(1)} %fusion.75), channel_id=1, source_target_pairs={{0,8},{4,12},{8,0},{12,4},{16,24},{20,28},{24,16},{28,20},{1,9},{5... | collective-permute-start | bytes 393224 | tf_op jit(solution)/shard_map/ppermute | solution.py:23
  35.6 5.1 %collective-permute-start.8 = (bf16[1,4,128,128]{2,3,1,0:T(8,128)(2,1)S(1)}, bf16[1,4,128,128]{2,3,1,0:T(8,128)(2,1)S(1)}, u32[]{:S(2)}, u32[]{:S(2)}) collective-permute-start(bf16[1,4,128,128]{2,3,1,0:T(8,128)(2,1)S(1)} %fusion.76), channel_id=1, source_target_pairs={{0,12},{4,8},{8,4},{12,0},{16,28},{20,24},{24,20},{28,16},{1,13},{... | collective-permute-start | bytes 393224 | tf_op jit(solution)/shard_map/ppermute | solution.py:23
  43.2 5.5 %collective-permute-start.10 = (bf16[128,1024]{1,0:T(8,128)(2,1)}, bf16[128,1024]{1,0:T(8,128)(2,1)}, u32[]{:S(2)}, u32[]{:S(2)}) collective-permute-start(bf16[128,1024]{1,0:T(8,128)(2,1)} %get-tuple-element.13), channel_id=1, source_target_pairs={{0,1},{1,0},{2,3},{3,2},{4,5},{5,4},{6,7},{7,6},{8,9},{9,8},{10,11... | collective-permute-start | bytes 786440 | tf_op jit(solution)/shard_map/ppermute | solution.py:23
  46.9 3.8 %collective-permute-start.9 = (bf16[128,1024]{1,0:T(8,128)(2,1)S(1)}, bf16[128,1024]{1,0:T(8,128)(2,1)}, u32[]{:S(2)}, u32[]{:S(2)}) collective-permute-start(bf16[128,1024]{1,0:T(8,128)(2,1)S(1)} %get-tuple-element.12), channel_id=1, source_target_pairs={{0,1},{1,0},{2,3},{3,2},{4,5},{5,4},{6,7},{7,6},{8,9},{9,8},{10,11... | collective-permute-start | bytes 786440 | tf_op jit(solution)/shard_map/ppermute | solution.py:23
  50.4 7.8 %collective-permute-start.11 = (bf16[128,1024]{1,0:T(8,128)(2,1)}, bf16[128,1024]{1,0:T(8,128)(2,1)}, u32[]{:S(2)}, u32[]{:S(2)}) collective-permute-start(bf16[128,1024]{1,0:T(8,128)(2,1)} %add_convert_fusion.1), channel_id=1, source_target_pairs={{0,2},{1,3},{2,0},{3,1},{4,6},{5,7},{6,4},{7,5},{8,10},{9,11},{10,... | collective-permute-start | bytes 786440 | tf_op jit(solution)/shard_map/ppermute | solution.py:23
  59.6 5.3 %copy-start.5 = (bf16[128,1024]{1,0:T(8,128)(2,1)}, bf16[128,1024]{1,0:T(8,128)(2,1)S(1)}, u32[]{:S(2)}) copy-start(bf16[128,1024]{1,0:T(8,128)(2,1)S(1)} %get-tuple-element.7.residual_ref) | copy-start | bytes 786436
  59.6 2.1 %collective-permute-start.12 = (f32[128]{0:T(128)S(1)}, f32[128]{0:T(128)S(1)}, u32[]{:S(2)}, u32[]{:S(2)}) collective-permute-start(f32[128]{0:T(128)S(1)} %get-tuple-element.6), channel_id=1, source_target_pairs={{0,1},{1,0},{2,3},{3,2},{4,5},{5,4},{6,7},{7,6},{8,9},{9,8},{10,11... | collective-permute-start | bytes 1544 | tf_op jit(solution)/shard_map/ppermute | solution.py:23
  61.7 2.4 %collective-permute-start.13 = (f32[128]{0:T(128)S(1)}, f32[128]{0:T(128)S(1)}, u32[]{:S(2)}, u32[]{:S(2)}) collective-permute-start(f32[128]{0:T(128)S(1)} %add.232), channel_id=1, source_target_pairs={{0,2},{1,3},{2,0},{3,1},{4,6},{5,7},{6,4},{7,5},{8,10},{9,11},{10,... | collective-permute-start | bytes 1544 | tf_op jit(solution)/shard_map/ppermute | solution.py:23
